TPU v7x, 32 devices: a whole 2x2x4 slice. The times are simulated.
32 devices in a mesh: rep: 2 (over y), seq: 8 (over z, x), head: 2 (over core).
Axes of the slice: x: 2, y: 2, z: 4, core: 2. Of those that a mesh axis runs over, the one named last changes fastest.
Arguments:
- x_in: bfloat16 [1024, 1024], P(('rep', 'seq'), 'head'), parts along dimension 0, may hold values from -6 to 6
- b_in: bfloat16 [1024, 2048], P(('rep', 'seq'), 'head'), parts along dimension 0, may hold values from -6 to 6
- c_in: bfloat16 [1024, 2048], P(('rep', 'seq'), 'head'), parts along dimension 0, may hold values from -6 to 6
- z_in: bfloat16 [1024, 1024], P(('rep', 'seq'), 'head'), parts along dimension 0, may hold values from -6 to 6
- dt_raw: bfloat16 [1024, 16], P(('rep', 'seq'), 'head'), parts along dimension 0, may hold values from -3 to 6
- dt_bias: float32 [16], P('head'), may hold values from -4 to -3
- a_log: float32 [16], P('head')
- d_skip: float32 [16], P('head'), may hold values from 0.5 to 1.5
- conv_x: bfloat16 [4, 1024], P(None, 'head'), may hold values from -3 to 3
- conv_b: bfloat16 [4, 2048], P(None, 'head'), may hold values from -3 to 3
- conv_c: bfloat16 [4, 2048], P(None, 'head'), may hold values from -3 to 3
- norm_gain: float32 [1024], P('head'), may hold values from 0.5 to 1.5
Outputs:
- mixed: bfloat16 [1024, 1024], P(('rep', 'seq'), 'head'), parts along dimension 0
There are 2 independent parts, one for each index of `rep`. A program takes and returns all parts, laid end to end along the dimension named above; an argument that names none is the same for every part. Nothing has to cross between parts.
All inputs are finite; a program needn't handle non-finite values.
Results may differ from a plain program's by a relative error of at most 0.0051.
Values may be sent and summed in bfloat16 or wider, within the bound.
A program may use at most 64 MiB of HBM per device.

v0:
```python
import jax
import jax.numpy as jnp
from jax import lax
from jax.sharding import PartitionSpec as P

HEAD_DIM = 64
STATE = 256
BLOCK = 256


def causal_conv(padded, kernel, length):
    summed = jnp.zeros((length,) + padded.shape[1:], jnp.float32)
    for offset in range(kernel.shape[0]):
        summed = summed + kernel[offset].astype(jnp.float32) * padded[
            offset : offset + length
        ].astype(jnp.float32)
    return jax.nn.silu(summed).astype(jnp.bfloat16)


def blockwise_scan(x_head, b_head, c_head, rates, decays):
    length = x_head.shape[0]
    blocks = length // BLOCK
    x_part = x_head.reshape(blocks, BLOCK, -1)
    b_part = b_head.reshape(blocks, BLOCK, -1)
    c_part = c_head.reshape(blocks, BLOCK, -1)
    rate_part = rates.reshape(blocks, BLOCK)
    log_decay = jnp.cumsum(decays.reshape(blocks, BLOCK), axis=1)
    causal = jnp.arange(BLOCK)[:, None] >= jnp.arange(BLOCK)[None, :]
    scores = jnp.einsum("cin,cjn->cij", c_part, b_part, preferred_element_type=jnp.float32)
    spread = jnp.where(causal, log_decay[:, :, None] - log_decay[:, None, :], 0.0)
    mixing = jnp.where(causal, scores * jnp.exp(spread) * rate_part[:, None, :], 0.0).astype(
        jnp.bfloat16
    )
    inner = jnp.einsum("cij,cjp->cip", mixing, x_part, preferred_element_type=jnp.float32)
    weighted_b = (
        b_part.astype(jnp.float32)
        * (jnp.exp(log_decay[:, -1:] - log_decay) * rate_part)[:, :, None]
    ).astype(jnp.bfloat16)
    block_states = jnp.einsum(
        "cjn,cjp->cnp", weighted_b, x_part, preferred_element_type=jnp.float32
    )
    totals = log_decay[:, -1]

    def carry_step(state, pair):
        total, fresh = pair
        return (jnp.exp(total) * state + fresh, state)

    final_state, entering = lax.scan(
        carry_step, jnp.zeros(block_states.shape[1:], jnp.float32), (totals, block_states)
    )
    entering_low = entering.astype(jnp.bfloat16)
    outer = jnp.exp(log_decay)[:, :, None] * jnp.einsum(
        "cin,cnp->cip", c_part, entering_low, preferred_element_type=jnp.float32
    )
    return (inner + outer).reshape(length, -1)


def body(x_in, b_in, c_in, z_in, dt_raw, dt_bias, a_log, d_skip, conv_x, conv_b, conv_c, norm_gain):
    local_rows = x_in.shape[0]
    seq_total = lax.axis_size("seq")
    seq_place = lax.axis_index("seq")
    heads_here = dt_raw.shape[1]
    per_device = heads_here // seq_total
    groups_here = b_in.shape[1] // STATE
    per_group = heads_here // groups_here
    kernel_taps = conv_x.shape[0]

    def widen(groupwise, last_dim):
        row_total = groupwise.shape[0]
        copies = jnp.broadcast_to(
            groupwise.reshape(row_total, groups_here, 1, last_dim),
            (row_total, groups_here, per_group, last_dim),
        )
        return copies.reshape(row_total, seq_total, per_device, last_dim)

    x_send, b_send, c_send = (x_in, b_in, c_in)
    outgoing = (
        x_send.reshape(local_rows, seq_total, per_device, HEAD_DIM),
        widen(b_send, STATE),
        widen(c_send, STATE),
        dt_raw.reshape(local_rows, seq_total, per_device),
    )
    arrived = (
        lax.all_to_all(outgoing[0], "seq", split_axis=1, concat_axis=0, tiled=True),
        lax.all_to_all(outgoing[1], "seq", split_axis=1, concat_axis=0, tiled=True),
        lax.all_to_all(outgoing[2], "seq", split_axis=1, concat_axis=0, tiled=True),
        lax.all_to_all(outgoing[3], "seq", split_axis=1, concat_axis=0, tiled=True),
    )
    length = local_rows * seq_total
    x_heads = arrived[0].reshape(length, per_device, HEAD_DIM)
    b_heads = arrived[1].reshape(length, per_device, STATE)
    c_heads = arrived[2].reshape(length, per_device, STATE)
    raw_rates = arrived[3].reshape(length, per_device)
    kernel_x = lax.dynamic_index_in_dim(
        conv_x.reshape(kernel_taps, seq_total, per_device, HEAD_DIM), seq_place, 1, keepdims=False
    )
    kernel_b = lax.dynamic_index_in_dim(widen(conv_b, STATE), seq_place, 1, keepdims=False)
    kernel_c = lax.dynamic_index_in_dim(widen(conv_c, STATE), seq_place, 1, keepdims=False)
    front = ((kernel_taps - 1, 0), (0, 0), (0, 0))
    x_heads = causal_conv(jnp.pad(x_heads, front), kernel_x, length)
    b_heads = causal_conv(jnp.pad(b_heads, front), kernel_b, length)
    c_heads = causal_conv(jnp.pad(c_heads, front), kernel_c, length)
    first_head = seq_place * per_device
    bias_here = lax.dynamic_slice_in_dim(dt_bias, first_head, per_device)
    alog_here = lax.dynamic_slice_in_dim(a_log, first_head, per_device)
    skip_here = lax.dynamic_slice_in_dim(d_skip, first_head, per_device)
    rates = jax.nn.softplus(raw_rates.astype(jnp.float32) + bias_here[None, :])
    decays = rates * (-jnp.exp(alog_here))[None, :]
    scanned = jax.vmap(blockwise_scan, in_axes=1, out_axes=1)(
        x_heads, b_heads, c_heads, rates, decays
    )
    heads_out = (scanned + skip_here[None, :, None] * x_heads.astype(jnp.float32)).astype(
        jnp.bfloat16
    )
    returned = lax.all_to_all(
        heads_out.reshape(length, 1, per_device, HEAD_DIM),
        "seq",
        split_axis=0,
        concat_axis=1,
        tiled=True,
    )
    merged = returned.reshape(local_rows, heads_here * HEAD_DIM).astype(jnp.float32)
    gated = merged * jax.nn.silu(z_in.astype(jnp.float32))
    grouped = gated.reshape(local_rows, groups_here, -1)
    mean_square = jnp.mean(grouped * grouped, axis=-1, keepdims=True)
    normed = (grouped * lax.rsqrt(mean_square + 1e-05)).reshape(local_rows, -1)
    return (normed * norm_gain[None, :]).astype(jnp.bfloat16)


def solution(mesh):
    placed = (
        P(("rep", "seq"), "head"),
        P(("rep", "seq"), "head"),
        P(("rep", "seq"), "head"),
        P(("rep", "seq"), "head"),
        P(("rep", "seq"), "head"),
        P("head"),
        P("head"),
        P("head"),
        P(None, "head"),
        P(None, "head"),
        P(None, "head"),
        P("head"),
    )
    return jax.shard_map(
        body, mesh=mesh, in_specs=placed, out_specs=P(("rep", "seq"), "head"), check_vma=False
    )
```

profile of v0, /device:TPU:0, one launch (start us, length us, event | category | flops | bytes accessed | tf_op | source)
XLA Modules:
  0.0 69.4 jit_solution(514059991303077825)
XLA Ops:
  0.0 1.3 %copy.99 = bf16[64,8,1]{0,2,1:T(2,128)(2,1)} copy(bf16[64,8,1]{0,1,2:T(8,128)(2,1)} %bitcast.160) | data formatting | bytes 2048 | tf_op jit(solution)/shard_map/reshape | solution.py:81
  1.3 7.3 %all-to-all-start.2 = ((bf16[64,8,1]{0,2,1:T(2,128)(2,1)}), bf16[64,8,1]{0,2,1:T(2,128)(2,1)S(1)}, u32[]{:S(2)}, u32[]{:S(2)}) async-start(bf16[64,8,1]{0,2,1:T(2,128)(2,1)} %copy.99), calls=%async_computation.2 | async-start | bytes 8192 | tf_op jit(solution)/shard_map/all_to_all | solution.py:87
  8.6 0.6 copy-done.4
  9.4 0.7 copy-done.6
  10.0 0.1 reshape.663
  10.2 0.6 copy-done.8
  10.8 0.6 dynamic_slice.30
  11.5 0.6 dynamic_slice.31
  12.8 0.8 %copy-done.3 = bf16[64,512]{1,0:T(8,128)(2,1)S(1)} copy-done((bf16[64,512]{1,0:T(8,128)(2,1)S(1)}, bf16[64,512]{1,0:T(8,128)(2,1)}, u32[]{:S(2)}) %copy-start.3) | copy-done | bytes 65560
  13.6 0.1 copy.103
  13.7 0.8 %reshape.665 = bf16[8,2,2048]{2,1,0:T(2,128)(2,1)} reshape(bf16[8,1,64,64]{3,2,1,0:T(8,128)(2,1)S(1)} %bitcast.145) | data formatting | bytes 131072
  14.5 0.1 copy-done.2
  14.7 0.6 copy-done.10
  15.3 0.6 dynamic_slice.33
  15.9 6.0 %all-to-all-start.3 = ((bf16[8,2,2048]{2,1,0:T(2,128)(2,1)}), bf16[8,2,2048]{2,1,0:T(2,128)(2,1)S(1)}, u32[]{:S(2)}, u32[]{:S(2)}) async-start(bf16[8,2,2048]{2,1,0:T(2,128)(2,1)} %reshape.665), calls=%async_computation.3 | async-start | bytes 131072 | tf_op jit(solution)/shard_map/all_to_all | solution.py:84
  21.9 0.6 convert_add_fusion
  22.5 0.1 add.166
  22.6 0.6 reduce-window.6
  23.2 0.2 slice_reduce_fusion
  23.4 0.1 copy.118
  23.5 0.1 add.168
  23.6 0.2 reduce-window.9
  23.8 0.1 copy.100
  24.0 4.8 %all-to-all-done.3 = bf16[8,2,2048]{2,1,0:T(2,128)(2,1)S(1)} async-done(((bf16[8,2,2048]{2,1,0:T(2,128)(2,1)}), bf16[8,2,2048]{2,1,0:T(2,128)(2,1)S(1)}, u32[]{:S(2)}, u32[]{:S(2)}) %all-to-all-start.3) | async-done | bytes 65568 | tf_op jit(solution)/shard_map/all_to_all | solution.py:84
  28.8 0.7 %broadcast_in_dim.82 = bf16[64,4,2,256]{3,0,2,1:T(8,128)(2,1)} broadcast(bf16[64,4,256]{2,0,1:T(8,128)(2,1)S(1)} %bitcast.144), dimensions={0,1,3} | broadcast | bytes 393216 | tf_op jit(solution)/shard_map/broadcast_in_dim | solution.py:70
  29.5 3.4 %all-to-all-start.1 = ((bf16[64,8,1,256]{3,0,2,1:T(8,128)(2,1)}), bf16[64,8,1,256]{3,0,2,1:T(8,128)(2,1)S(1)}, u32[]{:S(2)}, u32[]{:S(2)}) async-start(bf16[64,8,1,256]{3,0,2,1:T(8,128)(2,1)} %bitcast.12), calls=%async_computation.1 | async-start | bytes 524288 | tf_op jit(solution)/shard_map/all_to_all | solution.py:85
  33.0 0.2 reshape.666
  33.2 0.1 copy.104
  33.3 0.1 reshape.642
  33.4 0.2 multiply_convert_fusion.4
  33.6 7.5 %all-to-all-done.1 = bf16[64,8,1,256]{3,0,2,1:T(8,128)(2,1)S(1)} async-done(((bf16[64,8,1,256]{3,0,2,1:T(8,128)(2,1)}), bf16[64,8,1,256]{3,0,2,1:T(8,128)(2,1)S(1)}, u32[]{:S(2)}, u32[]{:S(2)}) %all-to-all-start.1) | async-done | bytes 262176 | tf_op jit(solution)/shard_map/all_to_all | solution.py:85
  41.1 0.7 %broadcast_in_dim.41 = bf16[64,4,2,256]{3,0,2,1:T(8,128)(2,1)} broadcast(bf16[64,4,256]{2,0,1:T(8,128)(2,1)S(1)} %bitcast.143), dimensions={0,1,3} | broadcast | bytes 393216 | tf_op jit(solution)/shard_map/broadcast_in_dim | solution.py:70
  41.8 3.4 %all-to-all-start = ((bf16[64,8,1,256]{3,0,2,1:T(8,128)(2,1)}), bf16[64,8,1,256]{3,0,2,1:T(8,128)(2,1)S(1)}, u32[]{:S(2)}, u32[]{:S(2)}) async-start(bf16[64,8,1,256]{3,0,2,1:T(8,128)(2,1)} %bitcast.1), calls=%async_computation | async-start | bytes 524288 | tf_op jit(solution)/shard_map/all_to_all | solution.py:86
  45.2 0.3 multiply_convert_fusion.1
  45.6 0.3 convolution_bitcast_fusion
  45.9 2.9 %while.13 = (s32[]{:T(128)}, f32[1,256,64]{2,1,0:T(8,128)S(1)}, bf16[2,1,256,64]{3,2,1,0:T(8,128)(2,1)S(1)}, f32[2,1]{0,1:T(1,128)S(1)}, f32[2,1,256,64]{2,3,0,1:T(8,128)S(1)}, /*index=5*/s32[]{:T(128)}, s32[]{:T(128)}) while((s32[]{:T(128)}, f32[1,256,64]{2,1,0:T(8,128)S(1)}, bf16[2,1,256,64]{3,2,1,0:T(8,128)(2,1)S(1)}, ...), condition=%wide.region_3.4_spmd.clone, body=%wide.region_2.3_spmd.clone.sunk | while | flops 65539 | bytes 655472 | solution.py:48
  45.9 0.1 copy.138
  46.0 0.6 fusion.52
  46.6 0.7 bitcast_add_fusion.4
  47.4 0.1 copy.138
  47.5 0.6 fusion.52
  48.1 0.7 bitcast_add_fusion.4
  48.8 4.6 %all-to-all-done = bf16[64,8,1,256]{3,0,2,1:T(8,128)(2,1)S(1)} async-done(((bf16[64,8,1,256]{3,0,2,1:T(8,128)(2,1)}), bf16[64,8,1,256]{3,0,2,1:T(8,128)(2,1)S(1)}, u32[]{:S(2)}, u32[]{:S(2)}) %all-to-all-start) | async-done | bytes 262176 | tf_op jit(solution)/shard_map/all_to_all | solution.py:86
  53.4 0.3 multiply_convert_fusion.2
  53.7 0.2 convolution_multiply_fusion.1
  54.0 0.4 fusion.4
  54.4 0.1 copy.110
  54.5 0.1 reshape.647
  54.6 0.8 %fusion.22 = bf16[512,1,1,64]{0,3,2,1:T(8,128)(2,1)S(1)} fusion(f32[512,1,64]{0,2,1:T(8,128)S(1)} %reshape.647, f32[]{:T(128)} %bitcast.43, bf16[512,1,64]{0,2,1:T(8,128)(2,1)S(1)} %reshape.642, f32[64]{0:T(128)S(1)} %get-tuple-element.105, f32[64]{0:T(128)S(1)} %get-tuple-element.103, f32[64]{0:T(128)S(1)} %get-tuple-element.104, f32[64]{0:T(128)S(1)} %get-tuple-element.102), kind=kLoop, calls=%fused_computation.45 | loop fusion | flops 655360 | bytes 263172 | tf_op jit(solution)/shard_map/reshape | solution.py:116
  55.4 0.5 broadcast.205
  55.9 0.7 reduce.2
  56.5 0.1 copy.136
  56.7 0.2 reshape.667
  56.8 9.6 %all_to_all.63 = bf16[8,2,2048]{2,1,0:T(2,128)(2,1)S(1)} all-to-all(bf16[8,2,2048]{2,1,0:T(2,128)(2,1)S(1)} %reshape.667), channel_id=1, replica_groups=mesh['rep'=2,'seq'=8,'head'=2] {'seq'}, dimensions={0} | all-to-all | bytes 131072 | tf_op jit(solution)/shard_map/all_to_all | solution.py:115
  66.4 0.1 reshape.668
  66.5 0.1 copy.112
  66.7 0.1 reshape.662
  66.8 0.2 copy.113
  67.0 0.1 reshape.661
  67.1 0.7 %copy-done = bf16[64,512]{1,0:T(8,128)(2,1)S(1)} copy-done((bf16[64,512]{1,0:T(8,128)(2,1)S(1)}, bf16[64,512]{1,0:T(8,128)(2,1)}, u32[]{:S(2)}) %copy-start) | copy-done | bytes 65560
  67.9 0.1 reduce_sum.9
  68.1 0.1 mul.289
  68.2 0.5 copy-done.7
  68.7 0.7 fusion.19
  (44 shorter events, 0.6 us)
Async XLA Ops:
  1.3 14.6 %all-to-all-start.2 = ((bf16[64,8,1]{0,2,1:T(2,128)(2,1)}), bf16[64,8,1]{0,2,1:T(2,128)(2,1)S(1)}, u32[]{:S(2)}, u32[]{:S(2)}) async-start(bf16[64,8,1]{0,2,1:T(2,128)(2,1)} %copy.99), calls=%async_computation.2 | async-start | bytes 8192 | tf_op jit(solution)/shard_map/all_to_all | solution.py:87
  8.5 0.7 %copy-start.4 = (bf16[4,1024]{1,0:T(4,128)(2,1)S(1)}, bf16[4,1024]{1,0:T(4,128)(2,1)}, u32[]{:S(2)}) copy-start(bf16[4,1024]{1,0:T(4,128)(2,1)} %param.24) | copy-start | bytes 24580
  8.5 0.7 %copy-start.5 = (bf16[4,1024]{1,0:T(4,128)(2,1)S(1)}, bf16[4,1024]{1,0:T(4,128)(2,1)}, u32[]{:S(2)}) copy-start(bf16[4,1024]{1,0:T(4,128)(2,1)} %param.23) | copy-start | bytes 24580
  8.6 4.2 %copy-start.1 = (bf16[64,1024]{1,0:T(8,128)(2,1)S(1)}, bf16[64,1024]{1,0:T(8,128)(2,1)}, u32[]{:S(2)}) copy-start(bf16[64,1024]{1,0:T(8,128)(2,1)} %param.15) | copy-start | bytes 393220
  9.3 0.7 copy-start.6
  10.2 0.7 copy-start.8
  10.8 0.7 copy-start.9
  12.8 0.8 %copy-start.3 = (bf16[64,512]{1,0:T(8,128)(2,1)S(1)}, bf16[64,512]{1,0:T(8,128)(2,1)}, u32[]{:S(2)}) copy-start(bf16[64,512]{1,0:T(8,128)(2,1)} %param.14) | copy-start | bytes 196612
  13.7 0.9 %copy-start.2 = (bf16[64,1024]{1,0:T(8,128)(2,1)S(1)}, bf16[64,1024]{1,0:T(8,128)(2,1)}, u32[]{:S(2)}) copy-start(bf16[64,1024]{1,0:T(8,128)(2,1)} %param.16) | copy-start | bytes 393220
  14.6 0.7 copy-start.10
  15.9 12.9 %all-to-all-start.3 = ((bf16[8,2,2048]{2,1,0:T(2,128)(2,1)}), bf16[8,2,2048]{2,1,0:T(2,128)(2,1)S(1)}, u32[]{:S(2)}, u32[]{:S(2)}) async-start(bf16[8,2,2048]{2,1,0:T(2,128)(2,1)} %reshape.665), calls=%async_computation.3 | async-start | bytes 131072 | tf_op jit(solution)/shard_map/all_to_all | solution.py:84
  29.5 11.6 %all-to-all-start.1 = ((bf16[64,8,1,256]{3,0,2,1:T(8,128)(2,1)}), bf16[64,8,1,256]{3,0,2,1:T(8,128)(2,1)S(1)}, u32[]{:S(2)}, u32[]{:S(2)}) async-start(bf16[64,8,1,256]{3,0,2,1:T(8,128)(2,1)} %bitcast.12), calls=%async_computation.1 | async-start | bytes 524288 | tf_op jit(solution)/shard_map/all_to_all | solution.py:85
  41.8 11.6 %all-to-all-start = ((bf16[64,8,1,256]{3,0,2,1:T(8,128)(2,1)}), bf16[64,8,1,256]{3,0,2,1:T(8,128)(2,1)S(1)}, u32[]{:S(2)}, u32[]{:S(2)}) async-start(bf16[64,8,1,256]{3,0,2,1:T(8,128)(2,1)} %bitcast.1), calls=%async_computation | async-start | bytes 524288 | tf_op jit(solution)/shard_map/all_to_all | solution.py:86
  66.9 0.8 %copy-start = (bf16[64,512]{1,0:T(8,128)(2,1)S(1)}, bf16[64,512]{1,0:T(8,128)(2,1)}, u32[]{:S(2)}) copy-start(bf16[64,512]{1,0:T(8,128)(2,1)} %param.17) | copy-start | bytes 196612
  68.0 0.7 copy-start.7
where the time goes:
time: 70.2 us; the launch traced here: 69.4 us
  starting transfers between devices  20.1 us (29%)
  waiting for transfers between devices  16.9 us (24%)
  local copies, waits for them, and re-layouts  14.7 us (21%)
  blocking collectives  9.55 us (14%)
  other arithmetic  6.17 us (9%)
  between operations  1.08 us (2%)
  matrix products  0.9 us (1%)
    all_to_all x1, blocking collectives, body(): lax.all_to_all(heads_out.reshape(length, 1, per_device, HEAD_DIM), 'seq',...  9.55 us
    all_to_all x1, waiting for transfers between devices, body(): lax.all_to_all(outgoing[1], 'seq', split_axis=1, concat_axis=0, tiled=True)  7.46 us
    all_to_all x1, starting transfers between devices, body(): lax.all_to_all(outgoing[3], 'seq', split_axis=1, concat_axis=0, tiled=True)  7.25 us
    unnamed x28, local copies, waits for them, and re-layouts  6.26 us
    all_to_all x1, starting transfers between devices, body(): lax.all_to_all(outgoing[0], 'seq', split_axis=1, concat_axis=0, tiled=True)  6 us
    all_to_all x1, waiting for transfers between devices, body(): lax.all_to_all(outgoing[0], 'seq', split_axis=1, concat_axis=0, tiled=True)  4.77 us
    all_to_all x1, waiting for transfers between devices, body(): lax.all_to_all(outgoing[2], 'seq', split_axis=1, concat_axis=0, tiled=True)  4.64 us
    all_to_all x1, starting transfers between devices, body(): lax.all_to_all(outgoing[1], 'seq', split_axis=1, concat_axis=0, tiled=True)  3.41 us
  transfers between devices with their start and end apart: 4, of which 3 were waited for; matrix products, arithmetic and copies ran while one was open for 13% of the time, Pallas kernels for 0%

commit v1 on v0

v1 whole, which is shorter than its diff:
```python
import functools

import jax
import jax.numpy as jnp
from jax import lax
from jax.experimental import pallas as pl
from jax.experimental.pallas import tpu as pltpu
from jax.sharding import PartitionSpec as P

HEAD_DIM = 64
STATE = 256
BLOCK = 256
LEAD = 16
PAIR = 2 * HEAD_DIM
NT = (((1,), (1,)), ((), ()))
TN = (((0,), (0,)), ((), ()))


def each(count, step):
    if count == 1:
        step(0)
    else:
        lax.fori_loop(0, count, lambda i, c: (step(i), c)[1], 0)


def aligned(index, unit):
    return pl.ds(pl.multiple_of(index * unit, unit), unit)


def conv_into(out_ref, buf_ref, taps_ref, rows, width):
    chunks = width // 128

    def lanes_step(k):
        lanes = aligned(k, 128)
        taps = taps_ref[:, lanes].astype(jnp.float32)
        count = taps.shape[0]
        for r in range(BLOCK // rows):
            part = buf_ref[r * rows : r * rows + rows + LEAD, lanes].astype(jnp.float32)
            total = taps[count - 1 : count] * part[LEAD:]
            for i in range(count - 1):
                total += taps[i : i + 1] * pltpu.roll(part, count - 1 - i, 0)[LEAD:]
            out_ref[r * rows : (r + 1) * rows, lanes] = jax.nn.silu(total).astype(jnp.bfloat16)

    if chunks <= 2:
        for k in range(chunks):
            lanes_step(k)
    else:
        each(chunks, lanes_step)


def kernel(
    blocks, members, rows, per_group, eps,
    x_hbm, b_hbm, c_hbm, z_hbm, dt_hbm, bias, alog, skip, tx_hbm, tb_hbm, tc_hbm, gain_hbm,
    out_ref,
    xbuf, bbuf, cbuf, dtbuf, zbuf, tx, tb, tc, gain,
    xconv, bconv, cconv, rowbuf, colbuf, acc, escale, enter, leave, outgoing, ret,
    local_sem, send_sem, recv_sem, halo_send, halo_recv, state_send, state_recv, ret_send, ret_recv,
):
    place = lax.axis_index("seq")
    me = lax.rem(place, members)
    block = place // members
    base = block * members
    width = per_group * HEAD_DIM
    pairs = per_group // 2
    high, low = me // 2, lax.rem(me, 2)

    def partner(d):
        return lax.rem(high + d // 2, 2) * 2 + lax.rem(low + d % 2, 2)

    def at(index):
        return {"seq": index}

    has_next = block < blocks - 1
    has_prev = block > 0
    is_last = me == members - 1

    barrier = pltpu.get_barrier_semaphore()
    for d in range(1, members):
        pl.semaphore_signal(barrier, inc=1, device_id=at(base + partner(d)))

    @pl.when(has_prev)
    def _():
        pl.semaphore_signal(barrier, inc=1, device_id=at(base - 1))

    @pl.when(jnp.logical_and(has_prev, jnp.logical_not(is_last)))
    def _():
        pl.semaphore_signal(barrier, inc=1, device_id=at(place - members))

    sources = (dt_hbm, x_hbm, b_hbm, c_hbm)
    buffers = (dtbuf, xbuf, bbuf, cbuf)
    widths = (None, width, STATE, STATE)

    def piece(n, group):
        if widths[n] is None:
            return sources[n]
        return sources[n].at[:, aligned(group, widths[n])]

    def slot(n, member):
        if widths[n] is None:
            return buffers[n].at[pl.ds(pl.multiple_of(member * rows, rows), rows)]
        return buffers[n].at[pl.ds(pl.multiple_of(member * rows + LEAD, LEAD), rows)]

    own = [pltpu.make_async_copy(piece(n, me), slot(n, me), local_sem.at[n]) for n in range(4)]
    small = [
        pltpu.make_async_copy(tx_hbm.at[:, aligned(me, width)], tx, local_sem.at[4]),
        pltpu.make_async_copy(tb_hbm.at[:, aligned(me, STATE)], tb, local_sem.at[5]),
        pltpu.make_async_copy(tc_hbm.at[:, aligned(me, STATE)], tc, local_sem.at[6]),
        pltpu.make_async_copy(gain_hbm, gain, local_sem.at[7]),
        pltpu.make_async_copy(z_hbm, zbuf, local_sem.at[8]),
    ]
    for copy in own + small:
        copy.start()

    @pl.when(jnp.logical_not(has_prev))
    def _():
        for buf in (xbuf, bbuf, cbuf):
            buf[0:LEAD] = jnp.zeros((LEAD, buf.shape[1]), jnp.bfloat16)
        enter[...] = jnp.zeros_like(enter)

    next_count = jnp.where(is_last, members, 1)
    pl.semaphore_wait(barrier, members - 1 + jnp.where(has_next, next_count, 0))

    sends = {}
    for n in range(4):
        for d in (3, 2, 1):
            sends[n, d] = pltpu.make_async_remote_copy(
                src_ref=piece(n, partner(d)),
                dst_ref=slot(n, me),
                send_sem=send_sem.at[n, d - 1],
                recv_sem=recv_sem.at[n, d - 1],
                device_id=at(base + partner(d)),
            )

    def halo(n, member):
        return pltpu.make_async_remote_copy(
            src_ref=sources[n].at[rows - LEAD : rows, aligned(member, widths[n])],
            dst_ref=buffers[n].at[0:LEAD],
            send_sem=halo_send.at[n - 1, member],
            recv_sem=halo_recv.at[n - 1],
            device_id=at(base + members + member),
        )

    sends_halo = jnp.logical_and(has_next, is_last)
    for n in range(4):
        for d in (3, 2, 1):
            sends[n, d].start()
        if n > 0:

            @pl.when(sends_halo)
            def _(n=n):
                for member in range(members):
                    halo(n, member).start()

    def arrive(n):
        own[n].wait()
        for d in (1, 2, 3):
            sends[n, d].wait_recv()
        if n > 0:

            @pl.when(has_prev)
            def _():
                halo(n, 0).wait_recv()

    arrive(0)
    raw = jnp.transpose(dtbuf[...].astype(jnp.float32))
    heads_here = raw.shape[0]
    head_id = lax.broadcasted_iota(jnp.int32, (heads_here, BLOCK), 0)
    sub = lax.broadcasted_iota(jnp.int32, (8, BLOCK), 0)
    up_to = (
        lax.broadcasted_iota(jnp.int32, (BLOCK, BLOCK), 0)
        <= lax.broadcasted_iota(jnp.int32, (BLOCK, BLOCK), 1)
    ).astype(jnp.float32).astype(jnp.bfloat16)

    def rates_step(p):
        first = me * per_group + 2 * p

        def row(k):
            return jnp.sum(jnp.where(head_id == first + k, raw, 0.0), axis=0, keepdims=True)

        def both(ref):
            return jnp.where(sub == 0, ref[first], ref[first + 1])

        v = jnp.where(sub == 0, row(0), row(1)) + both(bias)
        rates = jnp.maximum(v, 0.0) + jnp.log1p(jnp.exp(-jnp.abs(v)))
        decays = rates * -jnp.exp(both(alog))
        top = decays.astype(jnp.bfloat16).astype(jnp.float32)
        rest = decays - top
        middle = rest.astype(jnp.bfloat16).astype(jnp.float32)
        stacked = jnp.concatenate([top, middle, rest - middle, jnp.zeros_like(top)], axis=0)
        summed = jnp.dot(stacked.astype(jnp.bfloat16), up_to, preferred_element_type=jnp.float32)
        log_decay = summed[0:8] + summed[8:16] + summed[16:24]
        weight = jnp.exp(log_decay[:, BLOCK - 1 : BLOCK] - log_decay) * rates
        rowbuf[p, 0:8] = log_decay
        rowbuf[p, 8:16] = rates
        colbuf[p] = jnp.transpose(
            jnp.concatenate([log_decay, weight, jnp.exp(log_decay)], axis=0)
        )

    each(pairs, rates_step)

    first_half = lax.broadcasted_iota(jnp.int32, (BLOCK, PAIR), 1) < HEAD_DIM

    def spread(p, column):
        return jnp.where(
            first_half, colbuf[p, :, column : column + 1], colbuf[p, :, column + 1 : column + 2]
        )

    for copy in small[:3]:
        copy.wait()
    arrive(1)
    conv_into(xconv, xbuf, tx, rows, width)
    arrive(2)
    conv_into(bconv, bbuf, tb, rows, STATE)

    carry = pltpu.make_async_remote_copy(
        src_ref=leave,
        dst_ref=enter,
        send_sem=state_send,
        recv_sem=state_recv,
        device_id=at(place + members),
    )

    if blocks > 2:

        @pl.when(has_prev)
        def _():
            carry.wait_recv()

    @pl.when(has_next)
    def _():
        def state_step(p):
            scaled = (xconv[:, aligned(p, PAIR)].astype(jnp.float32) * spread(p, 8)).astype(
                jnp.bfloat16
            )
            fresh = lax.dot_general(scaled, bconv[...], TN, preferred_element_type=jnp.float32)
            if blocks > 2:
                total = jnp.exp(rowbuf[p, 0:8, BLOCK - 1 : BLOCK])
                upper = lax.broadcasted_iota(jnp.int32, (PAIR, STATE), 0) < HEAD_DIM
                fresh += jnp.where(upper, total[0:1], total[1:2]) * enter[aligned(p, PAIR)]
            leave[aligned(p, PAIR)] = fresh.astype(leave.dtype)

        each(pairs, state_step)
        carry.start()

    arrive(3)
    conv_into(cconv, cbuf, tc, rows, STATE)
    scores = lax.dot_general(cconv[...], bconv[...], NT, preferred_element_type=jnp.float32)
    causal = lax.broadcasted_iota(jnp.int32, (BLOCK, BLOCK), 0) >= lax.broadcasted_iota(
        jnp.int32, (BLOCK, BLOCK), 1
    )

    def inner_step(p):
        x_pair = xconv[:, aligned(p, PAIR)]
        x_wide = x_pair.astype(jnp.float32)
        first = me * per_group + 2 * p
        total = jnp.where(first_half, skip[first], skip[first + 1]) * x_wide
        for k in range(2):
            gap = colbuf[p, :, k : k + 1] - rowbuf[p, k : k + 1]
            mixing = jnp.where(
                causal,
                scores * jnp.exp(jnp.where(causal, gap, 0.0)) * rowbuf[p, 8 + k : 9 + k],
                0.0,
            ).astype(jnp.bfloat16)
            mine = first_half if k == 0 else jnp.logical_not(first_half)
            x_mine = jnp.where(mine, x_wide, 0.0).astype(jnp.bfloat16)
            total += jnp.dot(mixing, x_mine, preferred_element_type=jnp.float32)
        acc[:, aligned(p, PAIR)] = total
        escale[:, aligned(p, PAIR)] = spread(p, 16)

    each(pairs, inner_step)

    if blocks == 2:

        @pl.when(has_prev)
        def _():
            carry.wait_recv()

    returns = {}
    for d in (3, 2, 1, 0):
        target = partner(d)
        here = pl.ds(pl.multiple_of(target * rows, rows), rows)
        outer = lax.dot_general(
            cconv[here], enter[...].astype(jnp.bfloat16), NT, preferred_element_type=jnp.float32
        )
        result = (acc[here] + escale[here] * outer).astype(jnp.bfloat16)
        if d == 0:
            ret[me] = result
        else:
            outgoing[d - 1] = result
            returns[d] = pltpu.make_async_remote_copy(
                src_ref=outgoing.at[d - 1],
                dst_ref=ret.at[me],
                send_sem=ret_send.at[d - 1],
                recv_sem=ret_recv.at[d - 1],
                device_id=at(base + target),
            )
            returns[d].start()

    for copy in small[3:]:
        copy.wait()
    for n in range(4):
        for d in (1, 2, 3):
            sends[n, d].wait_send()

    @pl.when(sends_halo)
    def _():
        for n in (1, 2, 3):
            for member in range(members):
                halo(n, member).wait_send()

    @pl.when(has_next)
    def _():
        carry.wait_send()

    for d in (1, 2, 3):
        returns[d].wait_send()
        returns[d].wait_recv()

    for group in range(members):
        lanes = slice(group * width, (group + 1) * width)
        gated = ret[group].astype(jnp.float32) * jax.nn.silu(zbuf[:, lanes].astype(jnp.float32))
        mean_square = jnp.sum(gated * gated, axis=-1, keepdims=True) * (1.0 / width)
        out_ref[:, lanes] = (gated * lax.rsqrt(mean_square + eps) * gain[:, lanes]).astype(
            jnp.bfloat16
        )


def body(x_in, b_in, c_in, z_in, dt_raw, dt_bias, a_log, d_skip, conv_x, conv_b, conv_c, norm_gain):
    rows, channels = x_in.shape
    heads_here = dt_raw.shape[1]
    groups_here = b_in.shape[1] // STATE
    per_group = heads_here // groups_here
    members = BLOCK // rows
    blocks = lax.axis_size("seq") // members
    assert members == 4 and groups_here == members and per_group % 2 == 0
    width = per_group * HEAD_DIM
    pairs = per_group // 2
    taps = conv_x.shape[0]
    carried = jnp.bfloat16 if blocks == 2 else jnp.float32
    low, full = jnp.bfloat16, jnp.float32
    dma = pltpu.SemaphoreType.DMA
    hbm = pl.BlockSpec(memory_space=pl.ANY)
    smem = pl.BlockSpec(memory_space=pltpu.SMEM)
    return pl.pallas_call(
        functools.partial(kernel, blocks, members, rows, per_group, 1e-5),
        out_shape=jax.ShapeDtypeStruct((rows, channels), jnp.bfloat16),
        in_specs=[hbm] * 5 + [smem] * 3 + [hbm] * 4,
        out_specs=pl.BlockSpec(memory_space=pltpu.VMEM),
        scratch_shapes=[
            pltpu.VMEM((LEAD + BLOCK, width), low),
            pltpu.VMEM((LEAD + BLOCK, STATE), low),
            pltpu.VMEM((LEAD + BLOCK, STATE), low),
            pltpu.VMEM((BLOCK, heads_here), low),
            pltpu.VMEM((rows, channels), low),
            pltpu.VMEM((taps, width), low),
            pltpu.VMEM((taps, STATE), low),
            pltpu.VMEM((taps, STATE), low),
            pltpu.VMEM((1, channels), full),
            pltpu.VMEM((BLOCK, width), low),
            pltpu.VMEM((BLOCK, STATE), low),
            pltpu.VMEM((BLOCK, STATE), low),
            pltpu.VMEM((pairs, 16, BLOCK), full),
            pltpu.VMEM((pairs, BLOCK, 24), full),
            pltpu.VMEM((BLOCK, width), full),
            pltpu.VMEM((BLOCK, width), full),
            pltpu.VMEM((width, STATE), carried),
            pltpu.VMEM((width, STATE), carried),
            pltpu.VMEM((members - 1, rows, width), low),
            pltpu.VMEM((members, rows, width), low),
            dma((9,)),
            dma((4, 3)),
            dma((4, 3)),
            dma((3, members)),
            dma((3,)),
            dma,
            dma,
            dma((3,)),
            dma((3,)),
        ],
        compiler_params=pltpu.CompilerParams(
            collective_id=0, has_side_effects=True, vmem_limit_bytes=48 * 1024 * 1024
        ),
    )(
        x_in, b_in, c_in, z_in, dt_raw, dt_bias, a_log, d_skip,
        conv_x, conv_b, conv_c, norm_gain.reshape(1, channels),
    )


def solution(mesh):
    placed = (
        P(("rep", "seq"), "head"),
        P(("rep", "seq"), "head"),
        P(("rep", "seq"), "head"),
        P(("rep", "seq"), "head"),
        P(("rep", "seq"), "head"),
        P("head"),
        P("head"),
        P("head"),
        P(None, "head"),
        P(None, "head"),
        P(None, "head"),
        P("head"),
    )
    return jax.shard_map(
        body, mesh=mesh, in_specs=placed, out_specs=P(("rep", "seq"), "head"), check_vma=False
    )
```

time: 70.2 us -> 22.2 us (0.32)
  the two profiles are of different devices: /device:TPU:0 before, /device:TPU:16 now
where the time goes in v1:
time: 22.2 us; the launch traced here: 21.9 us
  Pallas kernels  16.1 us (73%)
  local copies, waits for them, and re-layouts  5.65 us (25%)
    pallas_call x1, Pallas kernels, body(): pl.pallas_call(functools.partial(kernel, blocks, members, rows, per_group...  16.1 us
    unnamed x24, local copies, waits for them, and re-layouts  5.65 us

profile of v1, /device:TPU:16, one launch (start us, length us, event | category | flops | bytes accessed | tf_op | source)
XLA Modules:
  0.0 21.9 jit_solution(14215622090164255877)
XLA Ops:
  0.0 0.0 copy-start.8
  0.0 0.0 copy-start.9
  0.0 0.0 copy-start.10
  0.0 0.0 copy-start.4
  0.0 0.0 copy-start.5
  0.0 0.0 copy-start.7
  0.0 0.8 %copy.13.dt_hbm = bf16[64,8]{1,0:T(8,128)(2,1)S(1)} copy(bf16[64,8]{0,1:T(8,128)(2,1)} %param.16) | data formatting | bytes 2048 | tf_op args[4]
  0.9 0.0 copy-done.8
  0.9 0.0 copy-done.9
  0.9 0.0 copy-done.10
  0.9 0.0 copy-done.4
  0.9 0.0 copy-done.5
  0.9 0.0 copy-done.7
  0.9 0.0 copy-start
  0.9 0.9 %copy-done = bf16[64,1024]{1,0:T(8,128)(2,1)S(1)} copy-done((bf16[64,1024]{1,0:T(8,128)(2,1)S(1)}, bf16[64,1024]{1,0:T(8,128)(2,1)}, u32[]{:S(2)}) %copy-start) | copy-done | bytes 131096
  1.8 0.0 copy-start.1
  1.8 0.9 %copy-done.1 = bf16[64,1024]{1,0:T(8,128)(2,1)S(1)} copy-done((bf16[64,1024]{1,0:T(8,128)(2,1)S(1)}, bf16[64,1024]{1,0:T(8,128)(2,1)}, u32[]{:S(2)}) %copy-start.1) | copy-done | bytes 131096
  2.7 0.0 copy-start.2
  2.7 0.8 %copy-done.2 = bf16[64,512]{1,0:T(8,128)(2,1)S(1)} copy-done((bf16[64,512]{1,0:T(8,128)(2,1)S(1)}, bf16[64,512]{1,0:T(8,128)(2,1)}, u32[]{:S(2)}) %copy-start.2) | copy-done | bytes 65560
  3.6 0.0 copy-start.3
  3.6 0.8 %copy-done.3 = bf16[64,512]{1,0:T(8,128)(2,1)S(1)} copy-done((bf16[64,512]{1,0:T(8,128)(2,1)S(1)}, bf16[64,512]{1,0:T(8,128)(2,1)}, u32[]{:S(2)}) %copy-start.3) | copy-done | bytes 65560
  4.4 0.0 copy-start.6
  4.4 0.7 %copy-done.6 = bf16[4,512]{1,0:T(4,128)(2,1)S(1)} copy-done((bf16[4,512]{1,0:T(4,128)(2,1)S(1)}, bf16[4,512]{1,0:T(4,128)(2,1)}, u32[]{:S(2)}) %copy-start.6) | copy-done | bytes 4120
  5.1 16.1 %shard_map.118 = bf16[64,512]{1,0:T(8,128)(2,1)S(1)} custom-call(bf16[64,512]{1,0:T(8,128)(2,1)S(1)} %copy-done.2, bf16[64,1024]{1,0:T(8,128)(2,1)S(1)} %copy-done, bf16[64,1024]{1,0:T(8,128)(2,1)S(1)} %copy-done.1, bf16[64,512]{1,0:T(8,128)(2,1)S(1)} %copy-done.3, bf16[64,8]{1,0:T(8,128)(2,1)S(1)} %copy.13.dt_hbm, f32[8]{0:T(128)S(1)} %copy-done.8, ...), custom_call_target="tpu_custom_call" | custom-call | tf_op jit(solution)/shard_map/pallas_call | solution.py:344
  21.2 0.6 %copy.15 = bf16[64,512]{1,0:T(8,128)(2,1)} copy(bf16[64,512]{1,0:T(8,128)(2,1)S(1)} %shard_map.118) | data formatting | bytes 131072
Async XLA Ops:
  0.0 0.9 %copy-start.8 = (f32[8]{0:T(128)S(1)}, f32[8]{0:T(128)}, u32[]{:S(2)}) copy-start(f32[8]{0:T(128)} %bias.1) | copy-start | bytes 100
  0.0 0.9 %copy-start.9 = (f32[8]{0:T(128)S(1)}, f32[8]{0:T(128)}, u32[]{:S(2)}) copy-start(f32[8]{0:T(128)} %alog.1) | copy-start | bytes 100
  0.0 0.9 %copy-start.10 = (f32[8]{0:T(128)S(1)}, f32[8]{0:T(128)}, u32[]{:S(2)}) copy-start(f32[8]{0:T(128)} %skip.1) | copy-start | bytes 100
  0.0 0.9 %copy-start.4 = (bf16[4,1024]{1,0:T(4,128)(2,1)S(1)}, bf16[4,1024]{1,0:T(4,128)(2,1)}, u32[]{:S(2)}) copy-start(bf16[4,1024]{1,0:T(4,128)(2,1)} %tb_hbm.1) | copy-start | bytes 24580
  0.0 0.9 %copy-start.5 = (bf16[4,1024]{1,0:T(4,128)(2,1)S(1)}, bf16[4,1024]{1,0:T(4,128)(2,1)}, u32[]{:S(2)}) copy-start(bf16[4,1024]{1,0:T(4,128)(2,1)} %tc_hbm.1) | copy-start | bytes 24580
  0.0 0.9 %copy-start.7 = (f32[512]{0:T(512)S(1)}, f32[512]{0:T(512)}, u32[]{:S(2)}) copy-start(f32[512]{0:T(512)} %param.23) | copy-start | bytes 6148
  0.9 0.9 %copy-start = (bf16[64,1024]{1,0:T(8,128)(2,1)S(1)}, bf16[64,1024]{1,0:T(8,128)(2,1)}, u32[]{:S(2)}) copy-start(bf16[64,1024]{1,0:T(8,128)(2,1)} %b_hbm.1) | copy-start | bytes 393220
  1.8 0.9 %copy-start.1 = (bf16[64,1024]{1,0:T(8,128)(2,1)S(1)}, bf16[64,1024]{1,0:T(8,128)(2,1)}, u32[]{:S(2)}) copy-start(bf16[64,1024]{1,0:T(8,128)(2,1)} %c_hbm.1) | copy-start | bytes 393220
  2.7 0.8 %copy-start.2 = (bf16[64,512]{1,0:T(8,128)(2,1)S(1)}, bf16[64,512]{1,0:T(8,128)(2,1)}, u32[]{:S(2)}) copy-start(bf16[64,512]{1,0:T(8,128)(2,1)} %x_hbm.1) | copy-start | bytes 196612
  3.6 0.8 %copy-start.3 = (bf16[64,512]{1,0:T(8,128)(2,1)S(1)}, bf16[64,512]{1,0:T(8,128)(2,1)}, u32[]{:S(2)}) copy-start(bf16[64,512]{1,0:T(8,128)(2,1)} %z_hbm.1) | copy-start | bytes 196612
  4.4 0.7 %copy-start.6 = (bf16[4,512]{1,0:T(4,128)(2,1)S(1)}, bf16[4,512]{1,0:T(4,128)(2,1)}, u32[]{:S(2)}) copy-start(bf16[4,512]{1,0:T(4,128)(2,1)} %tx_hbm.1) | copy-start | bytes 12292

commit v2 on v1

--- a/solution.py
+++ b/solution.py
@@ -25,6 +25,14 @@
 
 def aligned(index, unit):
     return pl.ds(pl.multiple_of(index * unit, unit), unit)
+
+
+def halo_spots(width):
+    return [(n, k) for n, w in enumerate((width, STATE, STATE)) for k in range(0, w, 128)]
+
+
+def halo_tiles(width):
+    return -(-len(halo_spots(width)) // 5)
 
 
 def conv_into(out_ref, buf_ref, taps_ref, rows, width):
@@ -50,9 +58,10 @@
 
 def kernel(
     blocks, members, rows, per_group, eps,
-    x_hbm, b_hbm, c_hbm, z_hbm, dt_hbm, bias, alog, skip, tx_hbm, tb_hbm, tc_hbm, gain_hbm,
+    x_hbm, b_hbm, c_hbm, z_hbm, dt_hbm, bias_hbm, alog_hbm, skip_hbm, tx_hbm, tb_hbm, tc_hbm, gain_hbm,
     out_ref,
-    xbuf, bbuf, cbuf, dtbuf, zbuf, tx, tb, tc, gain,
+    xbuf, bbuf, cbuf, dtbuf, zbuf, tx, tb, tc, gain, bias, alog, skip,
+    xtail, btail, ctail, packed, unpacked, gate,
     xconv, bconv, cconv, rowbuf, colbuf, acc, escale, enter, leave, outgoing, ret,
     local_sem, send_sem, recv_sem, halo_send, halo_recv, state_send, state_recv, ret_send, ret_recv,
 ):
@@ -97,7 +106,7 @@
 
     def slot(n, member):
         if widths[n] is None:
-            return buffers[n].at[pl.ds(pl.multiple_of(member * rows, rows), rows)]
+            return buffers[n].at[member]
         return buffers[n].at[pl.ds(pl.multiple_of(member * rows + LEAD, LEAD), rows)]
 
     own = [pltpu.make_async_copy(piece(n, me), slot(n, me), local_sem.at[n]) for n in range(4)]
@@ -107,7 +116,21 @@
         pltpu.make_async_copy(tc_hbm.at[:, aligned(me, STATE)], tc, local_sem.at[6]),
         pltpu.make_async_copy(gain_hbm, gain, local_sem.at[7]),
         pltpu.make_async_copy(z_hbm, zbuf, local_sem.at[8]),
+        pltpu.make_async_copy(bias_hbm, bias, local_sem.at[9]),
+        pltpu.make_async_copy(alog_hbm, alog, local_sem.at[10]),
+        pltpu.make_async_copy(skip_hbm, skip, local_sem.at[11]),
     ]
+    tails = [
+        pltpu.make_async_copy(hbm.at[rows - LEAD : rows], tail, local_sem.at[12 + k])
+        for k, (hbm, tail) in enumerate(((x_hbm, xtail), (b_hbm, btail), (c_hbm, ctail)))
+    ]
+    sends_halo = jnp.logical_and(has_next, is_last)
+
+    @pl.when(sends_halo)
+    def _():
+        for copy in tails:
+            copy.start()
+
     for copy in own + small:
         copy.start()
 
@@ -131,38 +154,60 @@
                 device_id=at(base + partner(d)),
             )
 
-    def halo(n, member):
+    def halo(member):
         return pltpu.make_async_remote_copy(
-            src_ref=sources[n].at[rows - LEAD : rows, aligned(member, widths[n])],
-            dst_ref=buffers[n].at[0:LEAD],
-            send_sem=halo_send.at[n - 1, member],
-            recv_sem=halo_recv.at[n - 1],
+            src_ref=packed.at[member],
+            dst_ref=unpacked,
+            send_sem=halo_send.at[member],
+            recv_sem=halo_recv,
             device_id=at(base + members + member),
         )
 
-    sends_halo = jnp.logical_and(has_next, is_last)
     for n in range(4):
         for d in (3, 2, 1):
             sends[n, d].start()
-        if n > 0:
-
-            @pl.when(sends_halo)
-            def _(n=n):
-                for member in range(members):
-                    halo(n, member).start()
+
+    spots = halo_spots(width)
+    inside = lax.broadcasted_iota(jnp.int32, (LEAD, 128), 0)
+
+    @pl.when(sends_halo)
+    def _():
+        for copy in tails:
+            copy.wait()
+        for member in range(members):
+            tile = jnp.zeros((LEAD, 128), jnp.float32)
+            for q, (n, start) in enumerate(spots):
+                place_in = 3 * (q % 5)
+                tail = (xtail, btail, ctail)[n]
+                offset = member * (width if n == 0 else STATE) + start
+                part = tail[:, offset : offset + 128].astype(jnp.float32)
+                part = pltpu.roll(part, (place_in + 3) % LEAD, 0)
+                fits = jnp.logical_and(inside >= place_in, inside < place_in + 3)
+                tile = jnp.where(fits, part, tile)
+                if q % 5 == 4 or q == len(spots) - 1:
+                    first = q // 5 * LEAD
+                    packed[member, first : first + LEAD] = tile.astype(jnp.bfloat16)
+            halo(member).start()
+
+    def take_halo():
+        @pl.when(has_prev)
+        def _():
+            halo(0).wait_recv()
+            for q, (n, start) in enumerate(spots):
+                first = q // 5 * LEAD
+                tile = unpacked[first : first + LEAD].astype(jnp.float32)
+                part = pltpu.roll(tile, (13 - 3 * (q % 5)) % LEAD, 0)
+                buffers[n + 1][0:LEAD, start : start + 128] = part.astype(jnp.bfloat16)
 
     def arrive(n):
         own[n].wait()
         for d in (1, 2, 3):
             sends[n, d].wait_recv()
-        if n > 0:
-
-            @pl.when(has_prev)
-            def _():
-                halo(n, 0).wait_recv()
 
     arrive(0)
-    raw = jnp.transpose(dtbuf[...].astype(jnp.float32))
+    raw = jnp.concatenate([dtbuf[m] for m in range(members)], axis=1).astype(jnp.float32)
+    for copy in small[5:]:
+        copy.wait()
     heads_here = raw.shape[0]
     head_id = lax.broadcasted_iota(jnp.int32, (heads_here, BLOCK), 0)
     sub = lax.broadcasted_iota(jnp.int32, (8, BLOCK), 0)
@@ -207,6 +252,7 @@
 
     for copy in small[:3]:
         copy.wait()
+    take_halo()
     arrive(1)
     conv_into(xconv, xbuf, tx, rows, width)
     arrive(2)
@@ -268,6 +314,12 @@
         escale[:, aligned(p, PAIR)] = spread(p, 16)
 
     each(pairs, inner_step)
+
+    for copy in small[3:5]:
+        copy.wait()
+    for group in range(members):
+        lanes = slice(group * width, (group + 1) * width)
+        gate[:, lanes] = jax.nn.silu(zbuf[:, lanes].astype(jnp.float32))
 
     if blocks == 2:
 
@@ -296,33 +348,32 @@
             )
             returns[d].start()
 
-    for copy in small[3:]:
-        copy.wait()
-    for n in range(4):
-        for d in (1, 2, 3):
-            sends[n, d].wait_send()
-
-    @pl.when(sends_halo)
-    def _():
-        for n in (1, 2, 3):
-            for member in range(members):
-                halo(n, member).wait_send()
-
-    @pl.when(has_next)
-    def _():
-        carry.wait_send()
-
-    for d in (1, 2, 3):
-        returns[d].wait_send()
-        returns[d].wait_recv()
-
-    for group in range(members):
-        lanes = slice(group * width, (group + 1) * width)
-        gated = ret[group].astype(jnp.float32) * jax.nn.silu(zbuf[:, lanes].astype(jnp.float32))
+    for d in (0, 1, 2, 3):
+        if d > 0:
+            returns[d].wait_recv()
+        group = partner(d)
+        lanes = aligned(group, width)
+        gated = ret[group].astype(jnp.float32) * gate[:, lanes]
         mean_square = jnp.sum(gated * gated, axis=-1, keepdims=True) * (1.0 / width)
         out_ref[:, lanes] = (gated * lax.rsqrt(mean_square + eps) * gain[:, lanes]).astype(
             jnp.bfloat16
         )
+
+    for n in range(4):
+        for d in (1, 2, 3):
+            sends[n, d].wait_send()
+
+    @pl.when(sends_halo)
+    def _():
+        for member in range(members):
+            halo(member).wait_send()
+
+    @pl.when(has_next)
+    def _():
+        carry.wait_send()
+
+    for d in (1, 2, 3):
+        returns[d].wait_send()
 
 
 def body(x_in, b_in, c_in, z_in, dt_raw, dt_bias, a_log, d_skip, conv_x, conv_b, conv_c, norm_gain):
@@ -335,27 +386,36 @@
     assert members == 4 and groups_here == members and per_group % 2 == 0
     width = per_group * HEAD_DIM
     pairs = per_group // 2
+    tiles = halo_tiles(width)
     taps = conv_x.shape[0]
     carried = jnp.bfloat16 if blocks == 2 else jnp.float32
     low, full = jnp.bfloat16, jnp.float32
     dma = pltpu.SemaphoreType.DMA
-    hbm = pl.BlockSpec(memory_space=pl.ANY)
-    smem = pl.BlockSpec(memory_space=pltpu.SMEM)
+    hbm = pl.BlockSpec(memory_space=pltpu.HBM)
     return pl.pallas_call(
         functools.partial(kernel, blocks, members, rows, per_group, 1e-5),
         out_shape=jax.ShapeDtypeStruct((rows, channels), jnp.bfloat16),
-        in_specs=[hbm] * 5 + [smem] * 3 + [hbm] * 4,
+        in_specs=[hbm] * 12,
         out_specs=pl.BlockSpec(memory_space=pltpu.VMEM),
         scratch_shapes=[
             pltpu.VMEM((LEAD + BLOCK, width), low),
             pltpu.VMEM((LEAD + BLOCK, STATE), low),
             pltpu.VMEM((LEAD + BLOCK, STATE), low),
-            pltpu.VMEM((BLOCK, heads_here), low),
+            pltpu.VMEM((members, heads_here, rows), low),
             pltpu.VMEM((rows, channels), low),
             pltpu.VMEM((taps, width), low),
             pltpu.VMEM((taps, STATE), low),
             pltpu.VMEM((taps, STATE), low),
             pltpu.VMEM((1, channels), full),
+            pltpu.SMEM((heads_here,), full),
+            pltpu.SMEM((heads_here,), full),
+            pltpu.SMEM((heads_here,), full),
+            pltpu.VMEM((LEAD, channels), low),
+            pltpu.VMEM((LEAD, b_in.shape[1]), low),
+            pltpu.VMEM((LEAD, b_in.shape[1]), low),
+            pltpu.VMEM((members, tiles * LEAD, 128), low),
+            pltpu.VMEM((tiles * LEAD, 128), low),
+            pltpu.VMEM((rows, channels), full),
             pltpu.VMEM((BLOCK, width), low),
             pltpu.VMEM((BLOCK, STATE), low),
             pltpu.VMEM((BLOCK, STATE), low),
@@ -367,21 +427,21 @@
             pltpu.VMEM((width, STATE), carried),
             pltpu.VMEM((members - 1, rows, width), low),
             pltpu.VMEM((members, rows, width), low),
-            dma((9,)),
+            dma((15,)),
             dma((4, 3)),
             dma((4, 3)),
-            dma((3, members)),
-            dma((3,)),
+            dma((members,)),
+            dma,
             dma,
             dma,
             dma((3,)),
             dma((3,)),
         ],
         compiler_params=pltpu.CompilerParams(
-            collective_id=0, has_side_effects=True, vmem_limit_bytes=48 * 1024 * 1024
+            collective_id=0, has_side_effects=True, vmem_limit_bytes=64 * 1024 * 1024
         ),
     )(
-        x_in, b_in, c_in, z_in, dt_raw, dt_bias, a_log, d_skip,
+        x_in, b_in, c_in, z_in, dt_raw.T, dt_bias, a_log, d_skip,
         conv_x, conv_b, conv_c, norm_gain.reshape(1, channels),
     )
 

time: 22.2 us -> 18.1 us (0.82)
  local copies, waits for them, and re-layouts: 5.65 us -> 1.47 us
  Pallas kernels: 16.1 us -> 16.4 us
    unnamed x24 -> x1, local copies, waits for them, and re-layouts: 5.65 us -> 1.47 us
    pallas_call x1, Pallas kernels: 16.1 us -> 16.4 us  [body(): pl.pallas_call(functools.partial(kernel, blocks, members, rows, per_group...]
where the time goes in v2:
time: 18.1 us; the launch traced here: 17.9 us
  Pallas kernels  16.4 us (91%)
  local copies, waits for them, and re-layouts  1.47 us (8%)
    pallas_call x1, Pallas kernels, body(): pl.pallas_call(functools.partial(kernel, blocks, members, rows, per_group...  16.4 us
    unnamed x1, local copies, waits for them, and re-layouts  1.47 us

profile of v2, /device:TPU:16, one launch (start us, length us, event | category | flops | bytes accessed | tf_op | source)
XLA Modules:
  0.0 17.9 jit_solution(5969632085386740257)
XLA Ops:
  0.0 16.4 %shard_map.118 = bf16[64,512]{1,0:T(8,128)(2,1)} custom-call(bf16[64,512]{1,0:T(8,128)(2,1)} %x_hbm.1, bf16[64,1024]{1,0:T(8,128)(2,1)} %b_hbm.1, bf16[64,1024]{1,0:T(8,128)(2,1)} %c_hbm.1, bf16[64,512]{1,0:T(8,128)(2,1)} %z_hbm.1, bf16[8,64]{1,0:T(8,128)(2,1)} %bitcast.2, f32[8]{0:T(128)} %bias_hbm.1, f32[8]{0:T(128)} %alog_hbm.1, f32[8]{0:T(128)} %skip_hbm.1, ...), custom_call_target="tpu_custom_call" | custom-call | tf_op jit(solution)/shard_map/pallas_call | solution.py:395
  16.4 1.5 %copy.14 = bf16[64,512]{1,0:T(8,128)(2,1)} copy(bf16[64,512]{1,0:T(8,128)(2,1)} %shard_map.118) | data formatting | bytes 131072

commit v3 on v2

--- a/solution.py
+++ b/solution.py
@@ -25,6 +25,11 @@
 
 def aligned(index, unit):
     return pl.ds(pl.multiple_of(index * unit, unit), unit)
+
+
+def silu(value):
+    half = 0.5 * value
+    return half * jnp.tanh(half) + half
 
 
 def halo_spots(width):
@@ -47,7 +52,7 @@
             total = taps[count - 1 : count] * part[LEAD:]
             for i in range(count - 1):
                 total += taps[i : i + 1] * pltpu.roll(part, count - 1 - i, 0)[LEAD:]
-            out_ref[r * rows : (r + 1) * rows, lanes] = jax.nn.silu(total).astype(jnp.bfloat16)
+            out_ref[r * rows : (r + 1) * rows, lanes] = silu(total).astype(jnp.bfloat16)
 
     if chunks <= 2:
         for k in range(chunks):
@@ -163,9 +168,16 @@
             device_id=at(base + members + member),
         )
 
-    for n in range(4):
+    def start(n):
         for d in (3, 2, 1):
             sends[n, d].start()
+
+    for n in range(3):
+        start(n)
+
+    @pl.when(jnp.logical_not(has_next))
+    def _():
+        start(3)
 
     spots = halo_spots(width)
     inside = lax.broadcasted_iota(jnp.int32, (LEAD, 128), 0)
@@ -256,6 +268,11 @@
     arrive(1)
     conv_into(xconv, xbuf, tx, rows, width)
     arrive(2)
+
+    @pl.when(has_next)
+    def _():
+        start(3)
+
     conv_into(bconv, bbuf, tb, rows, STATE)
 
     carry = pltpu.make_async_remote_copy(
@@ -290,27 +307,40 @@
 
     arrive(3)
     conv_into(cconv, cbuf, tc, rows, STATE)
-    scores = lax.dot_general(cconv[...], bconv[...], NT, preferred_element_type=jnp.float32)
-    causal = lax.broadcasted_iota(jnp.int32, (BLOCK, BLOCK), 0) >= lax.broadcasted_iota(
-        jnp.int32, (BLOCK, BLOCK), 1
-    )
+    half = BLOCK // 2
+    bands = []
+    for r in range(2):
+        span, reach = slice(r * half, (r + 1) * half), (r + 1) * half
+        scores = lax.dot_general(
+            cconv[span], bconv[0:reach], NT, preferred_element_type=jnp.float32
+        )
+        causal = lax.broadcasted_iota(jnp.int32, (half, reach), 0) + r * half >= (
+            lax.broadcasted_iota(jnp.int32, (half, reach), 1)
+        )
+        bands.append((span, reach, scores, causal))
 
     def inner_step(p):
         x_pair = xconv[:, aligned(p, PAIR)]
         x_wide = x_pair.astype(jnp.float32)
         first = me * per_group + 2 * p
-        total = jnp.where(first_half, skip[first], skip[first + 1]) * x_wide
-        for k in range(2):
-            gap = colbuf[p, :, k : k + 1] - rowbuf[p, k : k + 1]
-            mixing = jnp.where(
-                causal,
-                scores * jnp.exp(jnp.where(causal, gap, 0.0)) * rowbuf[p, 8 + k : 9 + k],
-                0.0,
-            ).astype(jnp.bfloat16)
-            mine = first_half if k == 0 else jnp.logical_not(first_half)
-            x_mine = jnp.where(mine, x_wide, 0.0).astype(jnp.bfloat16)
-            total += jnp.dot(mixing, x_mine, preferred_element_type=jnp.float32)
-        acc[:, aligned(p, PAIR)] = total
+        direct = jnp.where(first_half, skip[first], skip[first + 1]) * x_wide
+        x_mine = [
+            jnp.where(mine, x_wide, 0.0).astype(jnp.bfloat16)
+            for mine in (first_half, jnp.logical_not(first_half))
+        ]
+        for span, reach, scores, causal in bands:
+            total = direct[span]
+            for k in range(2):
+                gap = colbuf[p, span, k : k + 1] - rowbuf[p, k : k + 1, 0:reach]
+                mixing = jnp.where(
+                    causal,
+                    scores
+                    * jnp.exp(jnp.where(causal, gap, 0.0))
+                    * rowbuf[p, 8 + k : 9 + k, 0:reach],
+                    0.0,
+                ).astype(jnp.bfloat16)
+                total += jnp.dot(mixing, x_mine[k][0:reach], preferred_element_type=jnp.float32)
+            acc[span, aligned(p, PAIR)] = total
         escale[:, aligned(p, PAIR)] = spread(p, 16)
 
     each(pairs, inner_step)
@@ -319,7 +349,7 @@
         copy.wait()
     for group in range(members):
         lanes = slice(group * width, (group + 1) * width)
-        gate[:, lanes] = jax.nn.silu(zbuf[:, lanes].astype(jnp.float32))
+        gate[:, lanes] = silu(zbuf[:, lanes].astype(jnp.float32))
 
     if blocks == 2:
 
@@ -392,6 +422,13 @@
     low, full = jnp.bfloat16, jnp.float32
     dma = pltpu.SemaphoreType.DMA
     hbm = pl.BlockSpec(memory_space=pltpu.HBM)
+    operands = [
+        pltpu.with_memory_space_constraint(value, pltpu.HBM)
+        for value in (
+            x_in, b_in, c_in, z_in, dt_raw.T, dt_bias, a_log, d_skip,
+            conv_x, conv_b, conv_c, norm_gain.reshape(1, channels),
+        )
+    ]
     return pl.pallas_call(
         functools.partial(kernel, blocks, members, rows, per_group, 1e-5),
         out_shape=jax.ShapeDtypeStruct((rows, channels), jnp.bfloat16),
@@ -438,11 +475,10 @@
             dma((3,)),
         ],
         compiler_params=pltpu.CompilerParams(
-            collective_id=0, has_side_effects=True, vmem_limit_bytes=64 * 1024 * 1024
+            collective_id=0, has_side_effects=True, vmem_limit_bytes=32 * 1024 * 1024
         ),
     )(
-        x_in, b_in, c_in, z_in, dt_raw.T, dt_bias, a_log, d_skip,
-        conv_x, conv_b, conv_c, norm_gain.reshape(1, channels),
+        *operands,
     )
 
 

time: 18.1 us -> 17.8 us (0.983)
  the two profiles are of different devices: /device:TPU:16 before, /device:TPU:0 now
where the time goes in v3:
time: 17.8 us; the launch traced here: 17.7 us
  Pallas kernels  17 us (96%)
  local copies, waits for them, and re-layouts  0.63 us (4%)
    pallas_call x1, Pallas kernels, body(): pl.pallas_call(functools.partial(kernel, blocks, members, rows, per_group...  17 us
    unnamed x1, local copies, waits for them, and re-layouts  0.63 us

profile of v3, /device:TPU:0, one launch (start us, length us, event | category | flops | bytes accessed | tf_op | source)
XLA Modules:
  0.0 17.7 jit_solution(3977440695420117911)
XLA Ops:
  0.0 17.0 %shard_map.118 = bf16[64,512]{1,0:T(8,128)(2,1)S(1)} custom-call(bf16[64,512]{1,0:T(8,128)(2,1)} %x_hbm.1, bf16[64,1024]{1,0:T(8,128)(2,1)} %b_hbm.1, bf16[64,1024]{1,0:T(8,128)(2,1)} %c_hbm.1, bf16[64,512]{1,0:T(8,128)(2,1)} %z_hbm.1, bf16[8,64]{1,0:T(8,128)(2,1)} %bitcast.2, f32[8]{0:T(128)} %bias_hbm.1, f32[8]{0:T(128)} %alog_hbm.1, f32[8]{0:T(128)} %skip_hbm.1, ...), custom_call_target="tpu_custom_call" | custom-call | tf_op jit(solution)/shard_map/pallas_call | solution.py:432
  17.0 0.6 %copy.14 = bf16[64,512]{1,0:T(8,128)(2,1)} copy(bf16[64,512]{1,0:T(8,128)(2,1)S(1)} %shard_map.118) | data formatting | bytes 131072

commit v4 on v3

--- a/solution.py
+++ b/solution.py
@@ -67,7 +67,7 @@
     out_ref,
     xbuf, bbuf, cbuf, dtbuf, zbuf, tx, tb, tc, gain, bias, alog, skip,
     xtail, btail, ctail, packed, unpacked, gate,
-    xconv, bconv, cconv, rowbuf, colbuf, acc, escale, enter, leave, outgoing, ret,
+    xconv, bconv, cconv, rowbuf, colbuf, acc, escale, decay, enter, leave, outgoing, ret,
     local_sem, send_sem, recv_sem, halo_send, halo_recv, state_send, state_recv, ret_send, ret_recv,
 ):
     place = lax.axis_index("seq")
@@ -253,7 +253,14 @@
             jnp.concatenate([log_decay, weight, jnp.exp(log_decay)], axis=0)
         )
 
-    each(pairs, rates_step)
+    half = BLOCK // 2
+    bands = []
+    for r in range(2):
+        span, reach = slice(r * half, (r + 1) * half), (r + 1) * half
+        causal = lax.broadcasted_iota(jnp.int32, (half, reach), 0) + r * half >= (
+            lax.broadcasted_iota(jnp.int32, (half, reach), 1)
+        )
+        bands.append((span, reach, causal))
 
     first_half = lax.broadcasted_iota(jnp.int32, (BLOCK, PAIR), 1) < HEAD_DIM
 
@@ -261,18 +268,37 @@
         return jnp.where(
             first_half, colbuf[p, :, column : column + 1], colbuf[p, :, column + 1 : column + 2]
         )
+
+    def decay_step(p):
+        for span, reach, causal in bands:
+            for k in range(2):
+                gap = colbuf[p, span, k : k + 1] - rowbuf[p, k : k + 1, 0:reach]
+                decay[2 * p + k, span, 0:reach] = jnp.where(
+                    causal,
+                    jnp.exp(jnp.where(causal, gap, 0.0)) * rowbuf[p, 8 + k : 9 + k, 0:reach],
+                    0.0,
+                )
+        escale[:, aligned(p, PAIR)] = spread(p, 16)
+
+    each(pairs, rates_step)
+    each(pairs, decay_step)
+    for copy in small[3:5]:
+        copy.wait()
+    for group in range(members):
+        lanes = slice(group * width, (group + 1) * width)
+        gate[:, lanes] = silu(zbuf[:, lanes].astype(jnp.float32))
 
     for copy in small[:3]:
         copy.wait()
     take_halo()
     arrive(1)
+
+    @pl.when(has_next)
+    def _():
+        start(3)
+
     conv_into(xconv, xbuf, tx, rows, width)
     arrive(2)
-
-    @pl.when(has_next)
-    def _():
-        start(3)
-
     conv_into(bconv, bbuf, tb, rows, STATE)
 
     carry = pltpu.make_async_remote_copy(
@@ -307,17 +333,10 @@
 
     arrive(3)
     conv_into(cconv, cbuf, tc, rows, STATE)
-    half = BLOCK // 2
-    bands = []
-    for r in range(2):
-        span, reach = slice(r * half, (r + 1) * half), (r + 1) * half
-        scores = lax.dot_general(
-            cconv[span], bconv[0:reach], NT, preferred_element_type=jnp.float32
-        )
-        causal = lax.broadcasted_iota(jnp.int32, (half, reach), 0) + r * half >= (
-            lax.broadcasted_iota(jnp.int32, (half, reach), 1)
-        )
-        bands.append((span, reach, scores, causal))
+    scores = [
+        lax.dot_general(cconv[span], bconv[0:reach], NT, preferred_element_type=jnp.float32)
+        for span, reach, _ in bands
+    ]
 
     def inner_step(p):
         x_pair = xconv[:, aligned(p, PAIR)]
@@ -328,28 +347,14 @@
             jnp.where(mine, x_wide, 0.0).astype(jnp.bfloat16)
             for mine in (first_half, jnp.logical_not(first_half))
         ]
-        for span, reach, scores, causal in bands:
+        for score, (span, reach, _) in zip(scores, bands):
             total = direct[span]
             for k in range(2):
-                gap = colbuf[p, span, k : k + 1] - rowbuf[p, k : k + 1, 0:reach]
-                mixing = jnp.where(
-                    causal,
-                    scores
-                    * jnp.exp(jnp.where(causal, gap, 0.0))
-                    * rowbuf[p, 8 + k : 9 + k, 0:reach],
-                    0.0,
-                ).astype(jnp.bfloat16)
+                mixing = (score * decay[2 * p + k, span, 0:reach]).astype(jnp.bfloat16)
                 total += jnp.dot(mixing, x_mine[k][0:reach], preferred_element_type=jnp.float32)
             acc[span, aligned(p, PAIR)] = total
-        escale[:, aligned(p, PAIR)] = spread(p, 16)
 
     each(pairs, inner_step)
-
-    for copy in small[3:5]:
-        copy.wait()
-    for group in range(members):
-        lanes = slice(group * width, (group + 1) * width)
-        gate[:, lanes] = silu(zbuf[:, lanes].astype(jnp.float32))
 
     if blocks == 2:
 
@@ -357,26 +362,39 @@
         def _():
             carry.wait_recv()
 
-    returns = {}
-    for d in (3, 2, 1, 0):
-        target = partner(d)
-        here = pl.ds(pl.multiple_of(target * rows, rows), rows)
-        outer = lax.dot_general(
-            cconv[here], enter[...].astype(jnp.bfloat16), NT, preferred_element_type=jnp.float32
-        )
-        result = (acc[here] + escale[here] * outer).astype(jnp.bfloat16)
-        if d == 0:
-            ret[me] = result
-        else:
-            outgoing[d - 1] = result
-            returns[d] = pltpu.make_async_remote_copy(
-                src_ref=outgoing.at[d - 1],
-                dst_ref=ret.at[me],
-                send_sem=ret_send.at[d - 1],
-                recv_sem=ret_recv.at[d - 1],
-                device_id=at(base + target),
-            )
-            returns[d].start()
+    returns = {
+        d: pltpu.make_async_remote_copy(
+            src_ref=outgoing.at[d - 1],
+            dst_ref=ret.at[me],
+            send_sem=ret_send.at[d - 1],
+            recv_sem=ret_recv.at[d - 1],
+            device_id=at(base + partner(d)),
+        )
+        for d in (3, 2, 1)
+    }
+
+    def finish(with_outer):
+        for d in (3, 2, 1, 0):
+            here = pl.ds(pl.multiple_of(partner(d) * rows, rows), rows)
+            result = acc[here]
+            if with_outer:
+                result += escale[here] * lax.dot_general(
+                    cconv[here], enter[...].astype(jnp.bfloat16), NT,
+                    preferred_element_type=jnp.float32,
+                )
+            if d == 0:
+                ret[me] = result.astype(jnp.bfloat16)
+            else:
+                outgoing[d - 1] = result.astype(jnp.bfloat16)
+                returns[d].start()
+
+    @pl.when(has_prev)
+    def _():
+        finish(True)
+
+    @pl.when(jnp.logical_not(has_prev))
+    def _():
+        finish(False)
 
     for d in (0, 1, 2, 3):
         if d > 0:
@@ -460,6 +478,7 @@
             pltpu.VMEM((pairs, BLOCK, 24), full),
             pltpu.VMEM((BLOCK, width), full),
             pltpu.VMEM((BLOCK, width), full),
+            pltpu.VMEM((per_group, BLOCK, BLOCK), full),
             pltpu.VMEM((width, STATE), carried),
             pltpu.VMEM((width, STATE), carried),
             pltpu.VMEM((members - 1, rows, width), low),

time: 17.8 us -> 17.6 us (0.989)
  Pallas kernels: 17 us -> 16.8 us
    pallas_call x1, Pallas kernels: 17 us -> 16.8 us  [body(): pl.pallas_call(functools.partial(kernel, blocks, members, rows, per_group...]
where the time goes in v4:
time: 17.6 us; the launch traced here: 17.4 us
  Pallas kernels  16.8 us (95%)
  local copies, waits for them, and re-layouts  0.63 us (4%)
    pallas_call x1, Pallas kernels, body(): pl.pallas_call(functools.partial(kernel, blocks, members, rows, per_group...  16.8 us
    unnamed x1, local copies, waits for them, and re-layouts  0.63 us

profile of v4, /device:TPU:0, one launch (start us, length us, event | category | flops | bytes accessed | tf_op | source)
XLA Modules:
  0.0 17.4 jit_solution(3824971641042344860)
XLA Ops:
  0.0 16.8 %shard_map.118 = bf16[64,512]{1,0:T(8,128)(2,1)S(1)} custom-call(bf16[64,512]{1,0:T(8,128)(2,1)} %x_hbm.1, bf16[64,1024]{1,0:T(8,128)(2,1)} %b_hbm.1, bf16[64,1024]{1,0:T(8,128)(2,1)} %c_hbm.1, bf16[64,512]{1,0:T(8,128)(2,1)} %z_hbm.1, bf16[8,64]{1,0:T(8,128)(2,1)} %bitcast.2, f32[8]{0:T(128)} %bias_hbm.1, f32[8]{0:T(128)} %alog_hbm.1, f32[8]{0:T(128)} %skip_hbm.1, ...), custom_call_target="tpu_custom_call" | custom-call | tf_op jit(solution)/shard_map/pallas_call | solution.py:450
  16.8 0.6 %copy.14 = bf16[64,512]{1,0:T(8,128)(2,1)} copy(bf16[64,512]{1,0:T(8,128)(2,1)S(1)} %shard_map.118) | data formatting | bytes 131072

commit v5 on v4

--- a/solution.py
+++ b/solution.py
@@ -175,7 +175,9 @@
     for n in range(3):
         start(n)
 
-    @pl.when(jnp.logical_not(has_next))
+    yields = lax.axis_index("head") > 0
+
+    @pl.when(jnp.logical_not(yields))
     def _():
         start(3)
 
@@ -292,13 +294,13 @@
         copy.wait()
     take_halo()
     arrive(1)
-
-    @pl.when(has_next)
-    def _():
-        start(3)
-
     conv_into(xconv, xbuf, tx, rows, width)
     arrive(2)
+
+    @pl.when(yields)
+    def _():
+        start(3)
+
     conv_into(bconv, bbuf, tb, rows, STATE)
 
     carry = pltpu.make_async_remote_copy(

time: 17.6 us -> 16 us (0.909)
  the two profiles are of different devices: /device:TPU:0 before, /device:TPU:16 now
where the time goes in v5:
time: 16 us; the launch traced here: 15.8 us
  Pallas kernels  15.2 us (95%)
  local copies, waits for them, and re-layouts  0.63 us (4%)
    pallas_call x1, Pallas kernels, body(): pl.pallas_call(functools.partial(kernel, blocks, members, rows, per_group...  15.2 us
    unnamed x1, local copies, waits for them, and re-layouts  0.63 us

profile of v5, /device:TPU:16, one launch (start us, length us, event | category | flops | bytes accessed | tf_op | source)
XLA Modules:
  0.0 15.8 jit_solution(10744442948378694037)
XLA Ops:
  0.0 15.2 %shard_map.118 = bf16[64,512]{1,0:T(8,128)(2,1)S(1)} custom-call(bf16[64,512]{1,0:T(8,128)(2,1)} %x_hbm.1, bf16[64,1024]{1,0:T(8,128)(2,1)} %b_hbm.1, bf16[64,1024]{1,0:T(8,128)(2,1)} %c_hbm.1, bf16[64,512]{1,0:T(8,128)(2,1)} %z_hbm.1, bf16[8,64]{1,0:T(8,128)(2,1)} %bitcast.2, f32[8]{0:T(128)} %bias_hbm.1, f32[8]{0:T(128)} %alog_hbm.1, f32[8]{0:T(128)} %skip_hbm.1, ...), custom_call_target="tpu_custom_call" | custom-call | tf_op jit(solution)/shard_map/pallas_call | solution.py:452
  15.2 0.6 %copy.14 = bf16[64,512]{1,0:T(8,128)(2,1)} copy(bf16[64,512]{1,0:T(8,128)(2,1)S(1)} %shard_map.118) | data formatting | bytes 131072

commit v6 on v5

--- a/solution.py
+++ b/solution.py
@@ -40,7 +40,7 @@
     return -(-len(halo_spots(width)) // 5)
 
 
-def conv_into(out_ref, buf_ref, taps_ref, rows, width):
+def conv_into(out_ref, buf_ref, taps_ref, rows, width, only=None):
     chunks = width // 128
 
     def lanes_step(k):
@@ -54,7 +54,9 @@
                 total += taps[i : i + 1] * pltpu.roll(part, count - 1 - i, 0)[LEAD:]
             out_ref[r * rows : (r + 1) * rows, lanes] = silu(total).astype(jnp.bfloat16)
 
-    if chunks <= 2:
+    if only is not None:
+        lanes_step(only)
+    elif chunks <= 2:
         for k in range(chunks):
             lanes_step(k)
     else:
@@ -67,7 +69,7 @@
     out_ref,
     xbuf, bbuf, cbuf, dtbuf, zbuf, tx, tb, tc, gain, bias, alog, skip,
     xtail, btail, ctail, packed, unpacked, gate,
-    xconv, bconv, cconv, rowbuf, colbuf, acc, escale, decay, enter, leave, outgoing, ret,
+    xconv, bconv, cconv, rowbuf, colbuf, acc, escale, decay, scaled, enter, leave, outgoing, ret,
     local_sem, send_sem, recv_sem, halo_send, halo_recv, state_send, state_recv, ret_send, ret_recv,
 ):
     place = lax.axis_index("seq")
@@ -295,43 +297,57 @@
     take_halo()
     arrive(1)
     conv_into(xconv, xbuf, tx, rows, width)
+    def scale_step(p):
+        scaled[:, aligned(p, PAIR)] = (
+            xconv[:, aligned(p, PAIR)].astype(jnp.float32) * spread(p, 8)
+        ).astype(jnp.bfloat16)
+
+    each(pairs, scale_step)
     arrive(2)
 
     @pl.when(yields)
     def _():
         start(3)
 
-    conv_into(bconv, bbuf, tb, rows, STATE)
-
-    carry = pltpu.make_async_remote_copy(
-        src_ref=leave,
-        dst_ref=enter,
-        send_sem=state_send,
-        recv_sem=state_recv,
-        device_id=at(place + members),
-    )
-
-    if blocks > 2:
-
+    halves = [slice(k * 128, (k + 1) * 128) for k in range(STATE // 128)]
+    carries = [
+        pltpu.make_async_remote_copy(
+            src_ref=leave.at[:, lanes],
+            dst_ref=enter.at[:, lanes],
+            send_sem=state_send.at[k],
+            recv_sem=state_recv.at[k],
+            device_id=at(place + members),
+        )
+        for k, lanes in enumerate(halves)
+    ]
+
+    def take_states():
         @pl.when(has_prev)
         def _():
-            carry.wait_recv()
-
-    @pl.when(has_next)
-    def _():
-        def state_step(p):
-            scaled = (xconv[:, aligned(p, PAIR)].astype(jnp.float32) * spread(p, 8)).astype(
-                jnp.bfloat16
-            )
-            fresh = lax.dot_general(scaled, bconv[...], TN, preferred_element_type=jnp.float32)
-            if blocks > 2:
-                total = jnp.exp(rowbuf[p, 0:8, BLOCK - 1 : BLOCK])
-                upper = lax.broadcasted_iota(jnp.int32, (PAIR, STATE), 0) < HEAD_DIM
-                fresh += jnp.where(upper, total[0:1], total[1:2]) * enter[aligned(p, PAIR)]
-            leave[aligned(p, PAIR)] = fresh.astype(leave.dtype)
-
-        each(pairs, state_step)
-        carry.start()
+            for carry in carries:
+                carry.wait_recv()
+
+    if blocks > 2:
+        take_states()
+
+    for k, lanes in enumerate(halves):
+        conv_into(bconv, bbuf, tb, rows, STATE, k)
+
+        @pl.when(has_next)
+        def _(k=k, lanes=lanes):
+            def state_step(p):
+                fresh = lax.dot_general(
+                    scaled[:, aligned(p, PAIR)], bconv[:, lanes], TN,
+                    preferred_element_type=jnp.float32,
+                )
+                if blocks > 2:
+                    total = jnp.exp(rowbuf[p, 0:8, BLOCK - 1 : BLOCK])
+                    upper = lax.broadcasted_iota(jnp.int32, (PAIR, 128), 0) < HEAD_DIM
+                    fresh += jnp.where(upper, total[0:1], total[1:2]) * enter[aligned(p, PAIR), lanes]
+                leave[aligned(p, PAIR), lanes] = fresh.astype(leave.dtype)
+
+            each(pairs, state_step)
+            carries[k].start()
 
     arrive(3)
     conv_into(cconv, cbuf, tc, rows, STATE)
@@ -359,10 +375,7 @@
     each(pairs, inner_step)
 
     if blocks == 2:
-
-        @pl.when(has_prev)
-        def _():
-            carry.wait_recv()
+        take_states()
 
     returns = {
         d: pltpu.make_async_remote_copy(
@@ -420,7 +433,8 @@
 
     @pl.when(has_next)
     def _():
-        carry.wait_send()
+        for carry in carries:
+            carry.wait_send()
 
     for d in (1, 2, 3):
         returns[d].wait_send()
@@ -481,6 +495,7 @@
             pltpu.VMEM((BLOCK, width), full),
             pltpu.VMEM((BLOCK, width), full),
             pltpu.VMEM((per_group, BLOCK, BLOCK), full),
+            pltpu.VMEM((BLOCK, width), low),
             pltpu.VMEM((width, STATE), carried),
             pltpu.VMEM((width, STATE), carried),
             pltpu.VMEM((members - 1, rows, width), low),
@@ -490,8 +505,8 @@
             dma((4, 3)),
             dma((members,)),
             dma,
-            dma,
-            dma,
+            dma((2,)),
+            dma((2,)),
             dma((3,)),
             dma((3,)),
         ],

time: 16 us -> 15.9 us (level)
  no operation moved by 1% of the time
where the time goes in v6:
time: 15.9 us; the launch traced here: 15.7 us
  Pallas kernels  15.1 us (95%)
  local copies, waits for them, and re-layouts  0.63 us (4%)
    pallas_call x1, Pallas kernels, body(): pl.pallas_call(functools.partial(kernel, blocks, members, rows, per_group...  15.1 us
    unnamed x1, local copies, waits for them, and re-layouts  0.63 us

profile of v6, /device:TPU:16, one launch (start us, length us, event | category | flops | bytes accessed | tf_op | source)
XLA Modules:
  0.0 15.7 jit_solution(15093486341228222353)
XLA Ops:
  0.0 15.1 %shard_map.118 = bf16[64,512]{1,0:T(8,128)(2,1)S(1)} custom-call(bf16[64,512]{1,0:T(8,128)(2,1)} %x_hbm.1, bf16[64,1024]{1,0:T(8,128)(2,1)} %b_hbm.1, bf16[64,1024]{1,0:T(8,128)(2,1)} %c_hbm.1, bf16[64,512]{1,0:T(8,128)(2,1)} %z_hbm.1, bf16[8,64]{1,0:T(8,128)(2,1)} %bitcast.2, f32[8]{0:T(128)} %bias_hbm.1, f32[8]{0:T(128)} %alog_hbm.1, f32[8]{0:T(128)} %skip_hbm.1, ...), custom_call_target="tpu_custom_call" | custom-call | tf_op jit(solution)/shard_map/pallas_call | solution.py:466
  15.1 0.6 %copy.14 = bf16[64,512]{1,0:T(8,128)(2,1)} copy(bf16[64,512]{1,0:T(8,128)(2,1)S(1)} %shard_map.118) | data formatting | bytes 131072

commit v7 on v6

--- a/solution.py
+++ b/solution.py
@@ -305,10 +305,6 @@
     each(pairs, scale_step)
     arrive(2)
 
-    @pl.when(yields)
-    def _():
-        start(3)
-
     halves = [slice(k * 128, (k + 1) * 128) for k in range(STATE // 128)]
     carries = [
         pltpu.make_async_remote_copy(
@@ -348,6 +344,10 @@
 
             each(pairs, state_step)
             carries[k].start()
+
+    @pl.when(yields)
+    def _():
+        start(3)
 
     arrive(3)
     conv_into(cconv, cbuf, tc, rows, STATE)

time: 15.9 us -> 15.7 us (0.987)
  Pallas kernels: 15.1 us -> 14.9 us
where the time goes in v7:
time: 15.7 us; the launch traced here: 15.6 us
  Pallas kernels  14.9 us (95%)
  local copies, waits for them, and re-layouts  0.63 us (4%)
    pallas_call x1, Pallas kernels, body(): pl.pallas_call(functools.partial(kernel, blocks, members, rows, per_group...  14.9 us
    unnamed x1, local copies, waits for them, and re-layouts  0.63 us

profile of v7, /device:TPU:16, one launch (start us, length us, event | category | flops | bytes accessed | tf_op | source)
XLA Modules:
  0.0 15.6 jit_solution(15756119647926617750)
XLA Ops:
  0.0 14.9 %shard_map.118 = bf16[64,512]{1,0:T(8,128)(2,1)S(1)} custom-call(bf16[64,512]{1,0:T(8,128)(2,1)} %x_hbm.1, bf16[64,1024]{1,0:T(8,128)(2,1)} %b_hbm.1, bf16[64,1024]{1,0:T(8,128)(2,1)} %c_hbm.1, bf16[64,512]{1,0:T(8,128)(2,1)} %z_hbm.1, bf16[8,64]{1,0:T(8,128)(2,1)} %bitcast.2, f32[8]{0:T(128)} %bias_hbm.1, f32[8]{0:T(128)} %alog_hbm.1, f32[8]{0:T(128)} %skip_hbm.1, ...), custom_call_target="tpu_custom_call" | custom-call | tf_op jit(solution)/shard_map/pallas_call | solution.py:466
  15.0 0.6 %copy.14 = bf16[64,512]{1,0:T(8,128)(2,1)} copy(bf16[64,512]{1,0:T(8,128)(2,1)S(1)} %shard_map.118) | data formatting | bytes 131072
